TPU v7x, 32 devices: a whole 2x2x4 slice. The times are simulated.
32 devices in a mesh: groups: 2 (over x), clus: 16 (over z, y, core).
Axes of the slice: x: 2, y: 2, z: 4, core: 2. Of those that a mesh axis runs over, the one named last changes fastest.
Arguments:
- mesh_current: float32 [2, 131072], P(None, ('groups', 'clus')), parts along dimension 1, may hold values from -6 to 6
- branch_entry: int32 [2, 262144], P(None, ('groups', 'clus')), parts along dimension 1, may hold values from 0 to 6143, as said below
- branch_sign: int32 [2, 262144], P(None, ('groups', 'clus')), parts along dimension 1, may hold values from 0 to 1
- need_slots: int32 [512, 128], P(('groups', 'clus')), parts along dimension 0, may hold values from -1 to 4095, as said below
- resistance: float32 [262144], P(('groups', 'clus')), parts along dimension 0, may hold values from 0.3 to 3
- near_blocks: bfloat16 [2048, 4, 128, 128], P(('groups', 'clus')), parts along dimension 0, may hold values from -0.25 to 0.25
- near_source: int32 [2048, 4], P(('groups', 'clus')), parts along dimension 0, may hold values from 0 to 63
- basis_in: bfloat16 [2048, 32, 128], P(('groups', 'clus')), parts along dimension 0, may hold values from -0.5 to 0.5
- coupling: bfloat16 [2048, 16, 32, 32], P(('groups', 'clus')), parts along dimension 0, may hold values from -0.25 to 0.25
- basis_out: bfloat16 [2048, 32, 128], P(('groups', 'clus')), parts along dimension 0, may hold values from -1 to 1
- admissible: int32 [2048, 16], P(('groups', 'clus')), parts along dimension 0, may hold values from 0 to 1023, as said below
- port_mesh: int32 [128], P('groups'), parts along dimension 0, may hold values from 0 to 65535, as said below
- port_coupling: float32 [2, 64, 64], replicated, may hold values from -0.75 to 0.75
Outputs:
- mesh_voltage: float32 [2, 131072], P(None, ('groups', 'clus')), parts along dimension 1
There are 2 independent parts, one for each index of `groups`. A program takes and returns all parts, laid end to end along the dimension named above; an argument that names none is the same for every part. Nothing has to cross between parts.
Inputs may be any that keep to these rules, and one draw needn't show every extreme that they name: `need_slots`: row d * 16 + p holds distinct meshes of device p, counted from 0 within it, in its first slots and -1 in the rest. Row d * 16 + d is all -1; row d * 16 + (d + 1) % 16 has no -1. `branch_entry`: A value below 4096 is a mesh of the branch's own device d. Any other value is 4096 + p * 128 + s with p != d and slot s of row d * 16 + p of need_slots not -1. `admissible`: entry k of row t is (t + k * 64 + o) % 1024 with 1 <= o < 64; the entries of a row are distinct and never t. `port_mesh`: distinct meshes.
All inputs are finite; a program needn't handle non-finite values.
Results may differ from a plain program's by a relative error of at most 0.0021.
Values may be sent and summed in bfloat16 or wider, within the bound.
No kernel may reach another device: no remote copies, remote signals or barrier semaphores. Data moves between devices by JAX's collectives and lax.ppermute only.
A program may use at most 320 MiB of HBM per device.

v0:
```python
import functools
import math

import jax
import jax.numpy as jnp
from jax import lax
from jax.experimental import pallas as pl
from jax.experimental.pallas import tpu as pltpu
from jax.sharding import PartitionSpec as P

F32 = jnp.float32
BF16 = jnp.bfloat16
SPREAD = ("groups", "chips", "core")
STEPS = 32000.0
VMEM_LIMIT = 24 * 1024 * 1024
NT = (((1,), (1,)), ((), ()))


def params():
    return pltpu.CompilerParams(vmem_limit_bytes=VMEM_LIMIT)


def small_cost():
    return pl.CostEstimate(flops=10**9, bytes_accessed=8 * 10**6, transcendentals=0)


def lane_pick(row, lanes):
    spread = jnp.broadcast_to(row, lanes.shape)
    return jnp.take_along_axis(spread, lanes, axis=1, mode="promise_in_bounds")


def dot_nt(left, right, precision=None):
    return lax.dot_general(
        left, right, NT, preferred_element_type=F32, precision=precision
    )


def turn(members):
    return members // 4


def chip_turn(chips):
    return chips // 2


def by_place(rows):
    shift = chip_turn(rows.shape[0])
    return jnp.concatenate([rows[shift:], rows[:shift]], axis=0)


def device_index():
    return 2 * lax.axis_index("chips") + lax.axis_index("core")


def fetch(copies, late_copies):
    for copy in copies + late_copies:
        copy.start()
    for copy in copies:
        copy.wait()


def power_of_two(exponent):
    return jnp.exp(exponent * math.log(2.0))


def fixed(value):
    return jnp.floor(value + 0.5)


def pack_kernel(
    mesh_hbm, need_hbm, port_hbm, entry_hbm, sign_hbm, out_hbm, mesh_ref, need_ref, port_ref,
    code_ref, out_ref, stage_ref, entry_ref, sign_ref, sems,
):
    late_copies = [
        pltpu.make_async_copy(entry_hbm, entry_ref, sems.at[3]),
        pltpu.make_async_copy(sign_hbm, sign_ref, sems.at[4]),
    ]
    rows = mesh_ref.shape[1] // 128
    ports = port_ref.shape[1]
    chips = out_ref.shape[0]
    fetch(
        [
            pltpu.make_async_copy(source, target, sems.at[i])
            for i, (source, target) in enumerate(
                [(mesh_hbm, mesh_ref), (need_hbm, need_ref), (port_hbm, port_ref)]
            )
        ],
        late_copies,
    )
    for r in range(rows):
        stage_ref[r : r + 1, :] = mesh_ref[0:1, r * 128 : (r + 1) * 128]
        stage_ref[rows + r : rows + r + 1, :] = mesh_ref[1:2, r * 128 : (r + 1) * 128]
    block = stage_ref[...]
    largest = jnp.maximum(jnp.max(jnp.abs(block), axis=1, keepdims=True), 1e-30)
    largest = jnp.broadcast_to(largest, block.shape)
    exponent = jnp.ceil(jnp.log(largest) * (1.0 / math.log(2.0)))
    words = fixed(block * (power_of_two(-exponent) * STEPS)).astype(jnp.int32).astype(jnp.int16)
    top_exponent = jnp.max(exponent, axis=0, keepdims=True)
    unit = power_of_two(-top_exponent) * STEPS
    row_exponent = exponent.T[0:1]
    row_exponent = jnp.concatenate(
        [row_exponent, jnp.zeros((1, 128 - 2 * rows), F32)], axis=1
    )
    port = port_ref[...] - device_index() * (rows * 128)
    port = jnp.where((port >= 0) & (port < rows * 128), port, -1)
    port = jnp.broadcast_to(jnp.concatenate([port, port], axis=1), (8, 128))
    port_high, port_low = port >> 7, port & 127
    port_value = jnp.zeros((8, 128), F32)
    lane = lax.broadcasted_iota(jnp.int32, (8, 128), 1)
    for r in range(rows):
        real_row = stage_ref[r : r + 1, :]
        imag_row = stage_ref[rows + r : rows + r + 1, :]
        both = jnp.where(
            lane < ports, lane_pick(real_row, port_low), lane_pick(imag_row, port_low)
        )
        port_value = jnp.where(port_high == r, both, port_value)
    port_scaled = port_value[0:1] * unit
    port_top = fixed(port_scaled)
    port_rest = fixed((port_scaled - port_top) * STEPS)
    tail = [
        part.astype(jnp.int32) for part in (port_top, port_rest, row_exponent, top_exponent)
    ]
    tail.append(jnp.zeros((10, 128), jnp.int32))
    need = [by_place(need_ref[pl.ds(c, chips, 2), :]) for c in range(2)]
    first = lax.axis_index("core") == 0
    need = [jnp.where(first, need[0], need[1]), jnp.where(first, need[1], need[0])]
    for chip in range(chips):
        out_ref[chip, : 2 * rows, :] = words
        extra = [part[chip : chip + 1] for part in need] + tail
        out_ref[chip, 2 * rows :, :] = jnp.concatenate(extra, axis=0).astype(jnp.int16)
    out_copy = pltpu.make_async_copy(out_ref, out_hbm, sems.at[5])
    out_copy.start()
    for copy in late_copies:
        copy.wait()
    entry_ref[...] = entry_ref[...] * 2 + sign_ref[...]
    for k in range(2):
        for t in range(code_ref.shape[1]):
            code_ref[k, t : t + 1, :] = entry_ref[k : k + 1, t * 128 : (t + 1) * 128]
    out_copy.wait()


def hand_on_kernel(pack_hbm, part_hbm, out_hbm):
    pass


def extras(pack_ref, place, rows):
    extra = pack_ref[place, 2 * rows :, :].astype(jnp.int32)
    return extra, power_of_two(extra[4:6].astype(F32)) * (1.0 / STEPS)


def unpack_rows(pack_ref, rows_ref, request, rows):
    chips = pack_ref.shape[0]
    for chip in range(chips):
        place = (chip + chips - chip_turn(chips)) % chips
        extra, unit = extras(pack_ref, place, rows)
        extra = extra.astype(F32)
        rows_ref[0, chip : chip + 1, :] = extra[request : request + 1]
        rows_ref[1, chip : chip + 1, :] = (extra[2:3] + extra[3:4] * (1.0 / STEPS)) * unit[1:2]


def ask(need_ref, pack_ref, table_ref, core, rows):
    chips = pack_ref.shape[0]
    sub = lax.broadcasted_iota(jnp.int32, (rows, 128), 0)
    for chip in range(chips):
        place = (chip + chips - chip_turn(chips)) % chips
        wanted = need_ref[pl.ds(2 * chip + core, 1), :]
        wanted = jnp.broadcast_to(jnp.maximum(wanted, 0), (rows, 128))
        here = (wanted >> 7) == sub
        low = wanted & 127
        _, unit = extras(pack_ref, place, rows)
        row_of = (wanted >> 7)[0:8]
        for c in range(2):
            slot_unit = lane_pick(unit[0:1], row_of + c * rows)[0:1]
            block = pack_ref[place, c * rows : (c + 1) * rows, :].astype(jnp.int32).astype(F32)
            picked = jnp.take_along_axis(block, low, axis=1, mode="promise_in_bounds")
            picked = jnp.where(here, picked, 0.0)
            table_ref[c, chip : chip + 1, :] = slot_unit * jnp.sum(picked, axis=0, keepdims=True)


def lookup(code_ref, start, tables):
    total = [None, None]
    for k in range(2):
        code = code_ref[k, pl.ds(start, 8), :]
        high, low = code >> 8, (code >> 1) & 127
        value = [jnp.zeros((8, 128), F32), jnp.zeros((8, 128), F32)]
        for first, step, count, row_of in tables:
            offset = high - first
            for r in range(count):
                here = offset == r * step
                for c in range(2):
                    value[c] = jnp.where(here, lane_pick(row_of(r, c), low), value[c])
        along = (code & 1) == 1
        for c in range(2):
            signed = jnp.where(along, value[c], -value[c])
            total[c] = signed if k == 0 else total[c] + signed
    return total


def own_lookup_kernel(mesh_ref, code_ref, coupling_hbm, out_ref, pair_ref, raw_ref, sems):
    rows = mesh_ref.shape[1] // 128
    far_count, rank = coupling_hbm.shape[:2]
    half = rank // 2
    part = far_count // 2
    copies = [
        pltpu.make_async_copy(
            coupling_hbm.at[pl.ds(i * part, part)], raw_ref.at[pl.ds(i * part, part)], sems.at[i]
        )
        for i in range(2)
    ]
    for copy in copies:
        copy.start()

    def own_row(r, c):
        return mesh_ref[c : c + 1, r * 128 : (r + 1) * 128]

    def block(g, carry):
        start = pl.multiple_of(g * 8, 8)
        total = lookup(code_ref, start, [(0, 1, rows, own_row)])
        out_ref[0, pl.ds(start, 8), :] = total[0]
        out_ref[1, pl.ds(start, 8), :] = total[1]
        return carry

    lax.fori_loop(0, code_ref.shape[1] // 8, block, 0, unroll=True)
    for k in range(far_count):
        if k % part == 0:
            copies[k // part].wait()
        for r in range(half):
            pair_ref[k, r] = jnp.concatenate([raw_ref[k, r], raw_ref[k, half + r]], axis=1)


def add_peers(part_ref, pack_ref, need_ref, code_ref, table_ref, out_ref, core, first):
    chips = pack_ref.shape[0]
    ask(need_ref, pack_ref, table_ref, core, first)

    def peer_row(r, c):
        return table_ref[c, r : r + 1, :]

    def block(g, carry):
        start = pl.multiple_of(g * 8, 8)
        total = lookup(code_ref, start, [(first + core, 2, chips, peer_row)])
        for c in range(2):
            out_ref[c, pl.ds(start, 8), :] = total[c] + part_ref[c, pl.ds(start, 8), :]
        return carry

    lax.fori_loop(0, code_ref.shape[1] // 8, block, 0, unroll=True)


def same_core_kernel(
    part_ref, same_ref, need_ref, code_ref, out_ref, rows_ref, table_ref, *, first
):
    unpack_rows(same_ref, rows_ref, 0, first)
    add_peers(
        part_ref, same_ref, need_ref, code_ref, table_ref, out_ref,
        lax.axis_index("core"), first,
    )


def current_kernel(
    part_ref, other_ref, need_ref, code_ref, basis_hbm, current_ref, coeff_ref, rows_ref,
    table_ref, basis_ref, sem, *, first,
):
    tiles = code_ref.shape[1]
    rank = basis_ref.shape[0] // tiles
    copy = pltpu.make_async_copy(basis_hbm, basis_ref, sem.at[0])
    copy.start()
    unpack_rows(other_ref, rows_ref, 1, first)
    add_peers(
        part_ref, other_ref, need_ref, code_ref, table_ref, current_ref,
        1 - lax.axis_index("core"), first,
    )
    copy.wait()
    inputs = jnp.concatenate([current_ref[0], current_ref[1]], axis=0)
    inputs = inputs.T.astype(BF16)
    lane_tile = lax.broadcasted_iota(jnp.int32, (rank, 2 * tiles), 1) % tiles
    full = jnp.dot(basis_ref[...], inputs, preferred_element_type=F32)
    chosen = jnp.zeros((rank, 2 * tiles), F32)
    for t in range(tiles):
        chosen = jnp.where(lane_tile == t, full[t * rank : (t + 1) * rank], chosen)
    coeff = chosen.astype(BF16)
    for p in range(coeff_ref.shape[0]):
        coeff_ref[p] = coeff


def near_kernel(
    source_ref, current_ref, resistance_hbm, blocks_hbm, out_ref, inputs_ref, blocks_ref,
    resistance_ref, sems,
):
    tiles = current_ref.shape[1]
    width = blocks_ref.shape[1]
    count = blocks_ref.shape[0] // (tiles * width)
    span = 8 * count * width
    starts = [tiles * i // 64 for i in (0, 4, 8)]
    copies = {}
    for i in range(2):
        rows = pl.ds(starts[i] * span, (starts[i + 1] - starts[i]) * span)
        copies[starts[i]] = pltpu.make_async_copy(
            blocks_hbm.at[rows], blocks_ref.at[rows], sems.at[i]
        )
    late_copy = pltpu.make_async_copy(resistance_hbm, resistance_ref, sems.at[2])
    for copy in copies.values():
        copy.start()
    late_copy.start()
    lane_tile = lax.broadcasted_iota(jnp.int32, (width, 128), 1) % tiles
    rows = jnp.concatenate([current_ref[0], current_ref[1]], axis=0)
    columns = rows.T.astype(BF16)
    row_index = lax.broadcasted_iota(jnp.int32, (128, 128), 0)
    for k in range(count):
        picks = jnp.where(row_index == source_ref[k : k + 1, :], 1.0, 0.0).astype(BF16)
        inputs_ref[k * width : (k + 1) * width, :] = jnp.dot(
            columns, picks, preferred_element_type=F32
        ).astype(BF16)
    inputs = inputs_ref[...]
    total = jnp.zeros((width, 128), F32)
    for g in range(tiles // 8):
        if g in copies:
            copies[g].wait()
        block = jnp.concatenate(
            [
                jnp.concatenate(
                    [
                        blocks_ref[(t * count + k) * width : (t * count + k + 1) * width, :]
                        for t in range(g * 8, g * 8 + 8)
                    ],
                    axis=0,
                )
                for k in range(count)
            ],
            axis=1,
        )
        full = jnp.dot(block, inputs, preferred_element_type=F32)
        for i in range(8):
            total = jnp.where(
                lane_tile == g * 8 + i, full[i * width : (i + 1) * width], total
            )
    rows = total.T
    late_copy.wait()
    resistance = resistance_ref[...]
    out_ref[0] = resistance * current_ref[0] - rows[tiles:]
    out_ref[1] = resistance * current_ref[1] + rows[:tiles]


def split(value):
    top = value.astype(BF16)
    return top, (value - top.astype(F32)).astype(BF16)


def counts(rows):
    return lax.broadcasted_iota(jnp.int32, (rows, 128), 0).astype(F32)


def place(high, low, values, rows, spread_ref):
    sub_high, sub_low = counts(rows).astype(BF16), counts(128).astype(BF16)
    one, zero = jnp.ones((128, 128), BF16), jnp.zeros((128, 128), BF16)
    spread_ref[0] = high.astype(F32)
    spread_ref[1] = low.astype(F32)
    for c, value in enumerate(values):
        top, rest = split(value)
        spread_ref[2 + 2 * c] = top.astype(F32)
        spread_ref[3 + 2 * c] = rest.astype(F32)

    def spread(j, i, count):
        return jnp.broadcast_to(spread_ref[j, i : i + 1, :], (count, 128)).astype(BF16)

    left, right = [], []
    for i in range(8):
        here = spread(0, i, rows) == sub_high
        left.append(
            jnp.concatenate(
                [jnp.where(here, spread(j, i, rows), zero[:rows]) for j in range(2, 6)], axis=0
            )
        )
        right.append(jnp.where(spread(1, i, 128) == sub_low, one, zero))
    return jnp.concatenate(left, axis=1), jnp.concatenate(right, axis=1)


def place_few(high, low, values, rows):
    sub_high = lax.broadcasted_iota(jnp.int32, (rows, 128), 0)
    sub_low = lax.broadcasted_iota(jnp.int32, (128, 128), 0)
    left, right = [], []
    for i in range(high.shape[0]):
        here = jnp.broadcast_to(high[i : i + 1], (rows, 128)) == sub_high
        parts = []
        for value in values:
            spread = jnp.where(here, jnp.broadcast_to(value[i : i + 1], (rows, 128)), 0.0)
            parts.extend(split(spread))
        left.append(jnp.concatenate(parts, axis=0))
        there = jnp.broadcast_to(low[i : i + 1], (128, 128)) == sub_low
        right.append(jnp.where(there, 1.0, 0.0).astype(BF16))
    return jnp.concatenate(left, axis=1), jnp.concatenate(right, axis=1)


def scatter(code_ref, voltage_ref, spread_ref, first, rows, low_streams):
    total = None
    for g in range(code_ref.shape[1] // 8):
        for k in range(2):
            code = code_ref[k, g * 8 : g * 8 + 8, :]
            along = (code & 1) == 1
            values = []
            for c in range(2):
                voltage = voltage_ref[c, g * 8 : g * 8 + 8, :]
                values.append(jnp.where(along, voltage, -voltage))
            left, right = place(
                (code >> 8) - first, (code >> 1) & 127, values, rows, spread_ref.at[g, k]
            )
            term = dot_nt(right, left) if low_streams else dot_nt(left, right)
            total = term if total is None else total + term
    total = total.T if low_streams else total
    return [
        total[2 * c * rows : (2 * c + 1) * rows] + total[(2 * c + 1) * rows : (2 * c + 2) * rows]
        for c in range(2)
    ]


def voltage_kernel(
    coeff_ref, admissible_ref, coupling_ref, basis_ref, near_ref, code_ref, voltage_ref, slot_ref,
    picked_ref, mixed_ref, spread_ref, *, first,
):
    peers, rank, lanes = coeff_ref.shape
    far_count = coupling_ref.shape[0]
    tiles = lanes // 2
    half = rank // 2
    groups = half // 4
    device = device_index()
    all_tiles = peers * tiles
    band = all_tiles // far_count
    spans = band // tiles + 1
    stride = peers // far_count
    admissible = jnp.concatenate([admissible_ref[...], admissible_ref[...]], axis=1)
    window = lax.broadcasted_iota(jnp.int32, (far_count, lanes), 0) * band + device * tiles
    window = jnp.where(window >= all_tiles, window - all_tiles, window)
    shifted = admissible - window
    shifted = jnp.where(shifted < 0, shifted + all_tiles, shifted)
    component = lax.broadcasted_iota(jnp.int32, (rank, lanes), 1) // tiles
    for k in range(far_count):
        picked = jnp.zeros((rank, lanes), F32)
        for i in range(spans):
            block = coeff_ref[(device + k * stride + i + peers - turn(peers)) % peers].astype(F32)
            target = jnp.broadcast_to(shifted[k : k + 1] - i * tiles, (rank, lanes))
            source = jnp.clip(target, 0, tiles - 1) + component * tiles
            value = jnp.take_along_axis(block, source, axis=1, mode="promise_in_bounds")
            picked = jnp.where((target >= 0) & (target < tiles), value, picked)
        turned = pltpu.roll(picked, tiles, 1)
        picked_ref[0, k] = jnp.where(component == 0, picked, turned)
        picked_ref[1, k] = jnp.where(component == 0, turned, picked)

    def mix(g, carry):
        total = [[None, None] for _ in range(4)]
        for k in range(far_count):
            picked = [picked_ref[c, k] for c in range(2)]
            for i in range(4):
                block = coupling_ref[k, g * 4 + i].astype(F32)
                for c in range(2):
                    product = block * picked[c]
                    part = product[0:8]
                    for q in range(8, rank, 8):
                        part = part + product[q : q + 8]
                    total[i][c] = part if k == 0 else total[i][c] + part
        for i in range(4):
            for c in range(2):
                row = jnp.sum(total[i][c], axis=0, keepdims=True)
                mixed_ref[pl.ds(c * half + g * 4 + i, 1), :] = row
        return carry

    lax.fori_loop(0, groups, mix, 0, unroll=True)
    mixed = mixed_ref[...].T
    mixed = jnp.concatenate([mixed[:tiles], mixed[tiles:]], axis=1).astype(BF16)
    wide = 8 * rank
    from_row = lax.broadcasted_iota(jnp.int32, (2 * rank, wide), 0)
    to_rank = lax.broadcasted_iota(jnp.int32, (2 * rank, wide), 1) % rank
    repeated = []
    for c in range(2):
        wanted = (to_rank // half) * rank + c * half + to_rank % half
        picks = jnp.where(from_row == wanted, 1.0, 0.0).astype(BF16)
        repeated.append(jnp.dot(mixed, picks, preferred_element_type=F32))
    own_block = (
        lax.broadcasted_iota(jnp.int32, (16, wide), 0) % 8
        == lax.broadcasted_iota(jnp.int32, (16, wide), 1) // rank
    )
    for g in range(tiles // 8):
        rows8 = slice(g * 8, g * 8 + 8)
        both = jnp.concatenate([repeated[0][rows8], repeated[1][rows8]], axis=0)
        both = jnp.where(own_block, both, 0.0).astype(BF16)
        far = jnp.dot(
            both, basis_ref[g * wide : (g + 1) * wide, :], preferred_element_type=F32
        )
        voltage_ref[0, rows8, :] = near_ref[0, rows8, :] - far[8:16]
        voltage_ref[1, rows8, :] = near_ref[1, rows8, :] + far[0:8]
    sums = scatter(
        code_ref, voltage_ref, spread_ref, first, slot_ref.shape[0], True
    )
    shift = turn(peers)
    for c in range(2):
        slot_ref[: peers - shift, c, :] = sums[c][shift:]
        slot_ref[peers - shift :, c, :] = sums[c][:shift]


def own_sum_kernel(
    code_ref, voltage_ref, same_ref, other_ref, port_ref, impedance_ref, own_ref, asked_ref,
    picks_ref, spread_ref,
):
    rows = own_ref.shape[1]
    ports = impedance_ref.shape[1]
    chips = same_ref.shape[1]
    first_core = lax.axis_index("core") == 0
    same = same_ref[0].astype(jnp.int32)
    other = other_ref[0].astype(jnp.int32)
    asked = [jnp.where(first_core, same, other), jnp.where(first_core, other, same)]
    sub_low = lax.broadcasted_iota(jnp.int32, (128, 128), 0)
    for core in range(2):
        asked_ref[core] = asked[core] >> 7
        low = asked[core] & 127
        for chip in range(chips):
            there = jnp.broadcast_to(low[chip : chip + 1], (128, 128)) == sub_low
            place = core * chips + chip
            picks_ref[:, place * 128 : (place + 1) * 128] = jnp.where(there, 1.0, 0.0).astype(BF16)
    port_current = jnp.sum(same_ref[1] + other_ref[1], axis=0, keepdims=True)
    real = port_current[:, :ports]
    imag = port_current[:, ports:]
    both = jnp.concatenate([real, imag, jnp.zeros((6, ports), F32)], axis=0)
    by_real = dot_nt(both, impedance_ref[0], lax.Precision.HIGHEST)
    by_imag = dot_nt(both, impedance_ref[1], lax.Precision.HIGHEST)
    pad = jnp.zeros((1, 128 - ports), F32)
    terms = [
        jnp.concatenate([by_real[0:1] - by_imag[1:2], pad], axis=1),
        jnp.concatenate([by_real[1:2] + by_imag[0:1], pad], axis=1),
    ]
    port = port_ref[...] - device_index() * (rows * 128)
    port = jnp.where((port >= 0) & (port < rows * 128), port, -1)
    port = jnp.concatenate([port, jnp.full((1, 128 - ports), -1, jnp.int32)], axis=1)
    left, right = place_few(port >> 7, port & 127, terms, rows)
    total = dot_nt(left, right)
    sums = scatter(code_ref, voltage_ref, spread_ref, 0, rows, False)
    for c in range(2):
        own_ref[c] = sums[c] + (
            total[2 * c * rows : (2 * c + 1) * rows] + total[(2 * c + 1) * rows : (2 * c + 2) * rows]
        )


def finish_kernel(own_ref, arrived_ref, asked_ref, picks_ref, out_ref):
    rows = own_ref.shape[1]
    peers = arrived_ref.shape[0]
    chips = peers // 2
    sub_high = lax.broadcasted_iota(jnp.int32, (rows, 128), 0)
    left = []
    for core in range(2):
        for chip in range(chips):
            here = jnp.broadcast_to(asked_ref[core, chip : chip + 1, :], (rows, 128)) == sub_high
            parts = []
            for c in range(2):
                place = (2 * chip + core + peers - turn(peers)) % peers
                value = jnp.broadcast_to(arrived_ref[place, c : c + 1, :], (rows, 128))
                parts.extend(split(jnp.where(here, value, 0.0)))
            left.append(jnp.concatenate(parts, axis=0))
    total = dot_nt(jnp.concatenate(left, axis=1), picks_ref[...])
    for c in range(2):
        summed = own_ref[c] + (
            total[2 * c * rows : (2 * c + 1) * rows] + total[(2 * c + 1) * rows : (2 * c + 2) * rows]
        )
        for r in range(rows):
            out_ref[c : c + 1, r * 128 : (r + 1) * 128] = summed[r : r + 1]


def per_device(
    mesh_current,
    branch_entry,
    branch_sign,
    need_slots,
    resistance,
    near_blocks,
    near_source,
    basis_in,
    coupling,
    basis_out,
    admissible,
    port_mesh,
    port_coupling,
):
    chips = lax.axis_size("chips")
    peers = 2 * chips
    core = lax.axis_index("core")
    device = 2 * lax.axis_index("chips") + core
    mesh_dev = mesh_current.shape[1]
    tiles, near_count, width, _ = near_blocks.shape
    rank = basis_in.shape[1]
    far_count = admissible.shape[1]
    own_rows = mesh_dev // 128
    vmem = pl.BlockSpec(memory_space=pltpu.VMEM)
    shape = jax.ShapeDtypeStruct

    coupling_lanes = jnp.transpose(coupling, (1, 2, 3, 0))
    basis_in_rows = basis_in.reshape(tiles * rank, width)
    basis_out_rows = basis_out.reshape(tiles * rank, width)
    half = jnp.arange(2 * tiles, dtype=jnp.int32) // tiles
    sources = jnp.transpose(near_source)
    sources = jnp.concatenate([sources, sources], axis=1) + half[None] * tiles
    def in_hbm(x):
        return pltpu.with_memory_space_constraint(x, pltpu.HBM)

    hbm = pl.BlockSpec(memory_space=pl.ANY)
    port_row = port_mesh.reshape(1, -1)
    pack_rows = 2 * own_rows + 16
    pack_shape = (chips, pack_rows, 128)
    pack, mesh_near, need_near, port_near, code = pl.pallas_call(
        pack_kernel,
        out_shape=(
            pltpu.HBM(pack_shape, jnp.int16),
            pltpu.VMEM(mesh_current.shape, F32),
            pltpu.VMEM(need_slots.shape, jnp.int32),
            pltpu.VMEM(port_row.shape, jnp.int32),
            pltpu.VMEM((2, tiles, width), jnp.int32),
        ),
        in_specs=[hbm] * 5,
        out_specs=(hbm,) + (vmem,) * 4,
        scratch_shapes=[
            pltpu.VMEM(pack_shape, jnp.int16),
            pltpu.VMEM((2 * own_rows, 128), F32),
            pltpu.VMEM(branch_entry.shape, jnp.int32),
            pltpu.VMEM(branch_sign.shape, jnp.int32),
            pltpu.SemaphoreType.DMA((6,)),
        ],
        compiler_params=params(),
        name="pack",
    )(
        in_hbm(mesh_current),
        in_hbm(need_slots),
        in_hbm(port_row),
        in_hbm(branch_entry),
        in_hbm(branch_sign),
    )
    chip_members = [[(j + chip_turn(chips)) % chips for j in range(chips)]]
    same = lax.all_to_all(pack, "chips", 0, 0, tiled=True, axis_index_groups=chip_members)
    own_part, pairs = pl.pallas_call(
        own_lookup_kernel,
        out_shape=(
            shape((2, tiles, width), F32),
            pltpu.VMEM((far_count, rank // 2, rank, 2 * tiles), BF16),
        ),
        in_specs=[vmem] * 2 + [hbm],
        out_specs=(vmem,) * 2,
        scratch_shapes=[
            pltpu.VMEM(coupling_lanes.shape, BF16),
            pltpu.SemaphoreType.DMA((2,)),
        ],
        compiler_params=params(),
        cost_estimate=small_cost(),
        name="own_lookup",
    )(mesh_near, code, in_hbm(coupling_lanes))
    same = pl.pallas_call(
        hand_on_kernel,
        out_shape=shape(same.shape, same.dtype),
        in_specs=[hbm] * 2,
        out_specs=hbm,
        input_output_aliases={0: 0},
        compiler_params=params(),
        name="hand_on",
    )(same, own_part)
    other = lax.ppermute(same, "core", [(0, 1), (1, 0)])
    part, same_rows = pl.pallas_call(
        functools.partial(same_core_kernel, first=own_rows),
        out_shape=(shape((2, tiles, width), F32), shape((2, chips, 128), F32)),
        in_specs=[vmem] * 4,
        out_specs=(vmem,) * 2,
        scratch_shapes=[pltpu.VMEM((2, chips, 128), F32)],
        compiler_params=params(),
        cost_estimate=small_cost(),
        name="same_core",
    )(own_part, same, need_near, code)
    current, coeff, other_rows = pl.pallas_call(
        functools.partial(current_kernel, first=own_rows),
        out_shape=(
            shape((2, tiles, width), F32),
            shape((peers, rank, 2 * tiles), BF16),
            shape((2, chips, 128), F32),
        ),
        in_specs=[vmem] * 4 + [hbm],
        out_specs=(vmem,) * 3,
        scratch_shapes=[
            pltpu.VMEM((2, chips, 128), F32),
            pltpu.VMEM(basis_in_rows.shape, BF16),
            pltpu.SemaphoreType.DMA((1,)),
        ],
        compiler_params=params(),
        name="currents",
    )(part, other, need_near, code, in_hbm(basis_in_rows))
    members = [[(j + turn(peers)) % peers for j in range(peers)]]
    all_coeff = lax.all_to_all(
        coeff, ("chips", "core"), 0, 0, tiled=True, axis_index_groups=members
    )
    near_rows = near_blocks.reshape(tiles * near_count * width, width)
    near = pl.pallas_call(
        near_kernel,
        out_shape=shape((2, tiles, width), F32),
        in_specs=[vmem] * 2 + [hbm] * 2,
        out_specs=vmem,
        scratch_shapes=[
            pltpu.VMEM((near_count * width, 2 * tiles), BF16),
            pltpu.VMEM(near_rows.shape, BF16),
            pltpu.VMEM((tiles, width), F32),
            pltpu.SemaphoreType.DMA((3,)),
        ],
        compiler_params=params(),
        cost_estimate=pl.CostEstimate(
            flops=256 * near_blocks.size, bytes_accessed=2 * near_blocks.size, transcendentals=0
        ),
        name="near_field",
    )(sources, current, in_hbm(resistance.reshape(tiles, width)), in_hbm(near_rows))
    voltage, slots = pl.pallas_call(
        functools.partial(voltage_kernel, first=own_rows),
        out_shape=(shape((2, tiles, width), F32), shape((peers, 2, 128), F32)),
        in_specs=[vmem] * 6,
        out_specs=(vmem,) * 2,
        scratch_shapes=[
            pltpu.VMEM((2, far_count, rank, 2 * tiles), F32),
            pltpu.VMEM((rank, 2 * tiles), F32),
            pltpu.VMEM((tiles // 8, 2, 6, 8, 128), F32),
        ],
        compiler_params=params(),
        name="voltages",
    )(
        all_coeff,
        jnp.transpose(admissible),
        pairs,
        basis_out_rows,
        near,
        code,
    )
    arrived = lax.all_to_all(
        slots, ("chips", "core"), 0, 0, tiled=True, axis_index_groups=members
    )
    own, asked, picks = pl.pallas_call(
        own_sum_kernel,
        out_shape=(
            shape((2, own_rows, 128), F32),
            shape((2, chips, 128), jnp.int32),
            shape((128, peers * 128), BF16),
        ),
        in_specs=[vmem] * 6,
        out_specs=(vmem,) * 3,
        scratch_shapes=[
            pltpu.VMEM((tiles // 8, 2, 6, 8, 128), F32),
        ],
        compiler_params=params(),
        cost_estimate=small_cost(),
        name="own_sums",
    )(code, voltage, same_rows, other_rows, port_near, port_coupling)
    return pl.pallas_call(
        finish_kernel,
        out_shape=shape((2, mesh_dev), F32),
        in_specs=[vmem] * 4,
        out_specs=vmem,
        compiler_params=params(),
        name="finish",
    )(own, arrived, asked, picks)


def solution(mesh):
    groups, peers = mesh.devices.shape
    split_mesh = jax.sharding.Mesh(
        mesh.devices.reshape(groups, peers // 2, 2), ("groups", "chips", "core")
    )
    in_specs = (
        P(None, SPREAD),
        P(None, SPREAD),
        P(None, SPREAD),
        P(SPREAD, None),
        P(SPREAD),
        P(SPREAD, None, None, None),
        P(SPREAD, None),
        P(SPREAD, None, None),
        P(SPREAD, None, None, None),
        P(SPREAD, None, None),
        P(SPREAD, None),
        P("groups"),
        P(),
    )
    out_specs = P(None, SPREAD)
    return jax.shard_map(
        per_device, mesh=split_mesh, in_specs=in_specs, out_specs=out_specs, check_vma=False
    )
```

profile of v0, /device:TPU:0, one launch (start us, length us, event | category | flops | bytes accessed | tf_op | source)
XLA Modules:
  0.0 42.3 jit_solution(202944543139532850)
XLA Ops:
  0.0 1.8 %pack.1 = (s16[8,80,128]{2,1,0:T(8,128)(2,1)}, f32[2,4096]{1,0:T(2,128)S(1)}, s32[16,128]{1,0:T(8,128)S(1)}, s32[1,64]{1,0:T(1,128)S(1)}, s32[2,64,128]{2,1,0:T(8,128)S(1)}) custom-call(f32[2,4096]{1,0:T(2,128)} %mesh_hbm.1, s32[16,128]{1,0:T(8,128)} %need_hbm.1, s32[1,64]{1,0:T(1,128)} %bitcast.15, s32[2,8192]{1,0:T(2,128)} %entry_hbm.1, s32[2,8192]{1,0:T(2,128)} %sign_hbm.1), custom_call_target="tpu_custom_call" | custom-call | tf_op jit(solution)/shard_map/pack/pallas_call | solution.py:603
  1.8 7.9 %all-to-all-start = ((s16[8,80,128]{2,1,0:T(8,128)(2,1)}), s16[8,80,128]{2,1,0:T(8,128)(2,1)S(1)}, u32[]{:S(2)}, u32[]{:S(2)}) async-start(s16[8,80,128]{2,1,0:T(8,128)(2,1)} %get-tuple-element.25), calls=%async_computation | async-start | bytes 327680 | tf_op jit(solution)/shard_map/all_to_all | solution.py:631
  9.6 0.0 copy-start.3
  9.6 3.7 %own_lookup.1 = (f32[2,64,128]{2,1,0:T(8,128)S(1)}, bf16[16,16,32,128]{3,2,1,0:T(8,128)(2,1)S(1)}) custom-call(f32[2,4096]{1,0:T(2,128)S(1)} %get-tuple-element.23.mesh_ref, s32[2,64,128]{2,1,0:T(8,128)S(1)} %get-tuple-element.22.code_ref, bf16[16,32,32,64]{3,2,1,0:T(8,128)(2,1)} %bitcast.11), custom_call_target="tpu_custom_call" | custom-call | flops 1000000000 | bytes 8000000 | tf_op jit(solution)/shard_map/own_lookup/pallas_call | solution.py:632
  13.3 1.5 %all-to-all-done.pack_hbm = s16[8,80,128]{2,1,0:T(8,128)(2,1)S(1)} async-done(((s16[8,80,128]{2,1,0:T(8,128)(2,1)}), s16[8,80,128]{2,1,0:T(8,128)(2,1)S(1)}, u32[]{:S(2)}, u32[]{:S(2)}) %all-to-all-start) | async-done | bytes 163872 | tf_op jit(solution)/shard_map/all_to_all | solution.py:631
  14.8 0.0 collective-permute-start
  14.8 0.6 %same_core.1 = (f32[2,64,128]{2,1,0:T(8,128)S(1)}, f32[2,8,128]{2,1,0:T(8,128)S(1)}) custom-call(f32[2,64,128]{2,1,0:T(8,128)S(1)} %get-tuple-element.24.part_hbm.part_ref, s16[8,80,128]{2,1,0:T(8,128)(2,1)S(1)} %hand_on.1.same_ref, s32[16,128]{1,0:T(8,128)S(1)} %get-tuple-element.26.need_ref, s32[2,64,128]{2,1,0:T(8,128)S(1)} %get-tuple-element.22.code_ref), custom_call_target="tpu_custom_call" | custom-call | flops 1000000000 | bytes 8000000 | tf_op jit(solution)/shard_map/same_core/pallas_call | solution.py:658
  15.5 0.8 %collective-permute-done.other_ref = s16[8,80,128]{2,1,0:T(8,128)(2,1)S(1)} collective-permute-done((s16[8,80,128]{2,1,0:T(8,128)(2,1)S(1)}, s16[8,80,128]{2,1,0:T(8,128)(2,1)S(1)}, u32[]{:S(2)}, u32[]{:S(2)}) %collective-permute-start) | collective-permute-done | bytes 163872 | tf_op jit(solution)/shard_map/ppermute | solution.py:657
  16.2 2.1 %currents.1 = (f32[2,64,128]{2,1,0:T(8,128)S(1)}, bf16[16,32,128]{2,1,0:T(8,128)(2,1)}, f32[2,8,128]{2,1,0:T(8,128)S(1)}) custom-call(f32[2,64,128]{2,1,0:T(8,128)S(1)} %get-tuple-element.27.part_ref, s16[8,80,128]{2,1,0:T(8,128)(2,1)S(1)} %collective-permute-done.other_ref, s32[16,128]{1,0:T(8,128)S(1)} %get-tuple-element.26.need_ref, ...), custom_call_target="tpu_custom_call" | custom-call | tf_op jit(solution)/shard_map/currents/pallas_call | solution.py:668
  18.4 4.2 %all-to-all-start.1 = ((bf16[16,32,128]{2,1,0:T(8,128)(2,1)}), bf16[16,32,128]{2,1,0:T(8,128)(2,1)S(1)}, u32[]{:S(2)}, u32[]{:S(2)}) async-start(bf16[16,32,128]{2,1,0:T(8,128)(2,1)} %get-tuple-element.28), calls=%async_computation.1 | async-start | bytes 262144 | tf_op jit(solution)/shard_map/all_to_all | solution.py:686
  22.6 0.0 copy-done.3
  22.6 0.1 add_add_fusion.source_ref
  22.7 0.0 copy-start
  22.7 0.0 copy-start.1
  22.7 0.0 copy-start.2
  22.7 4.9 %near_field.1.near_ref = f32[2,64,128]{2,1,0:T(8,128)S(1)} custom-call(s32[4,128]{1,0:T(4,128)S(1)} %add_add_fusion.source_ref, f32[2,64,128]{2,1,0:T(8,128)S(1)} %get-tuple-element.30.current_ref, f32[64,128]{1,0:T(8,128)} %bitcast.13, bf16[32768,128]{1,0:T(8,128)(2,1)} %bitcast.10), custom_call_target="tpu_custom_call" | custom-call | flops 1073741824 | bytes 8388608 | tf_op jit(solution)/shard_map/near_field/pallas_call | solution.py:690
  27.5 1.6 %all-to-all-done.1.coeff_ref = bf16[16,32,128]{2,1,0:T(8,128)(2,1)S(1)} async-done(((bf16[16,32,128]{2,1,0:T(8,128)(2,1)}), bf16[16,32,128]{2,1,0:T(8,128)(2,1)S(1)}, u32[]{:S(2)}, u32[]{:S(2)}) %all-to-all-start.1) | async-done | bytes 131104 | tf_op jit(solution)/shard_map/all_to_all | solution.py:686
  29.1 0.0 copy-done
  29.1 0.0 copy-done.1
  29.1 3.5 %voltages.1 = (f32[2,64,128]{2,1,0:T(8,128)S(1)}, f32[16,2,128]{2,1,0:T(2,128)}) custom-call(bf16[16,32,128]{2,1,0:T(8,128)(2,1)S(1)} %all-to-all-done.1.coeff_ref, s32[16,64]{1,0:T(8,128)S(1)} %bitcast.9, bf16[16,16,32,128]{3,2,1,0:T(8,128)(2,1)S(1)} %get-tuple-element.29.coupling_ref, bf16[2048,128]{1,0:T(8,128)(2,1)S(1)} %bitcast.8, ...), custom_call_target="tpu_custom_call" | custom-call | tf_op jit(solution)/shard_map/voltages/pallas_call | solution.py:707
  32.7 3.6 %all-to-all-start.2 = ((f32[16,2,128]{2,1,0:T(2,128)}), f32[16,2,128]{2,1,0:T(2,128)S(1)}, u32[]{:S(2)}, u32[]{:S(2)}) async-start(f32[16,2,128]{2,1,0:T(2,128)} %get-tuple-element.36), calls=%async_computation.2 | async-start | bytes 32768 | tf_op jit(solution)/shard_map/all_to_all | solution.py:727
  36.2 0.0 copy-done.2
  36.2 1.6 %own_sums.1 = (f32[2,32,128]{2,1,0:T(8,128)S(1)}, s32[2,8,128]{2,1,0:T(8,128)S(1)}, bf16[128,2048]{1,0:T(8,128)(2,1)S(1)}) custom-call(s32[2,64,128]{2,1,0:T(8,128)S(1)} %get-tuple-element.22.code_ref, f32[2,64,128]{2,1,0:T(8,128)S(1)} %get-tuple-element.31.voltage_ref, f32[2,8,128]{2,1,0:T(8,128)S(1)} %get-tuple-element.32.same_ref, ...), custom_call_target="tpu_custom_call" | custom-call | flops 1000000000 | bytes 8000000 | tf_op jit(solution)/shard_map/own_sums/pallas_call | solution.py:730
  37.8 3.5 %all-to-all-done.2.arrived_ref = f32[16,2,128]{2,1,0:T(2,128)S(1)} async-done(((f32[16,2,128]{2,1,0:T(2,128)}), f32[16,2,128]{2,1,0:T(2,128)S(1)}, u32[]{:S(2)}, u32[]{:S(2)}) %all-to-all-start.2) | async-done | bytes 16416 | tf_op jit(solution)/shard_map/all_to_all | solution.py:727
  41.3 0.9 %finish.1 = f32[2,4096]{1,0:T(2,128)} custom-call(f32[2,32,128]{2,1,0:T(8,128)S(1)} %get-tuple-element.35.own_ref, f32[16,2,128]{2,1,0:T(2,128)S(1)} %all-to-all-done.2.arrived_ref, s32[2,8,128]{2,1,0:T(8,128)S(1)} %get-tuple-element.37.asked_ref, bf16[128,2048]{1,0:T(8,128)(2,1)S(1)} %get-tuple-element.38.picks_ref), custom_call_target="tpu_custom_call" | custom-call | tf_op jit(solution)/shard_map/finish/pallas_call | solution.py:746
  (2 shorter events, 0.0 us)
Async XLA Ops:
  1.8 13.1 %all-to-all-start = ((s16[8,80,128]{2,1,0:T(8,128)(2,1)}), s16[8,80,128]{2,1,0:T(8,128)(2,1)S(1)}, u32[]{:S(2)}, u32[]{:S(2)}) async-start(s16[8,80,128]{2,1,0:T(8,128)(2,1)} %get-tuple-element.25), calls=%async_computation | async-start | bytes 327680 | tf_op jit(solution)/shard_map/all_to_all | solution.py:631
  9.6 12.9 %copy-start.3 = (s32[64,4]{0,1:T(4,128)S(1)}, s32[64,4]{0,1:T(4,128)}, u32[]{:S(2)}) copy-start(s32[64,4]{0,1:T(4,128)} %param.19) | copy-start | bytes 3076
  14.8 1.4 %collective-permute-start = (s16[8,80,128]{2,1,0:T(8,128)(2,1)S(1)}, s16[8,80,128]{2,1,0:T(8,128)(2,1)S(1)}, u32[]{:S(2)}, u32[]{:S(2)}) collective-permute-start(s16[8,80,128]{2,1,0:T(8,128)(2,1)S(1)} %hand_on.1.same_ref), channel_id=1, source_target_pairs={{0,1},{1,0},{2,3},{3,2},{4,5},{5,4},{6,7},{7,6},{8,9},{9,8},{10,11... | collective-permute-start | bytes 491528 | tf_op jit(solution)/shard_map/ppermute | solution.py:657
  18.4 10.8 %all-to-all-start.1 = ((bf16[16,32,128]{2,1,0:T(8,128)(2,1)}), bf16[16,32,128]{2,1,0:T(8,128)(2,1)S(1)}, u32[]{:S(2)}, u32[]{:S(2)}) async-start(bf16[16,32,128]{2,1,0:T(8,128)(2,1)} %get-tuple-element.28), calls=%async_computation.1 | async-start | bytes 262144 | tf_op jit(solution)/shard_map/all_to_all | solution.py:686
  22.7 6.5 %copy-start = (bf16[64,32,128]{2,1,0:T(8,128)(2,1)S(1)}, bf16[64,32,128]{2,1,0:T(8,128)(2,1)}, u32[]{:S(2)}) copy-start(bf16[64,32,128]{2,1,0:T(8,128)(2,1)} %param.22) | copy-start | bytes 1572868
  22.7 6.5 %copy-start.1 = (s32[64,16]{0,1:T(8,128)S(1)}, s32[64,16]{0,1:T(8,128)}, u32[]{:S(2)}) copy-start(s32[64,16]{0,1:T(8,128)} %param.23) | copy-start | bytes 12292
  22.7 13.6 %copy-start.2 = (f32[2,64,64]{2,1,0:T(8,128)S(1)}, f32[2,64,64]{2,1,0:T(8,128)}, u32[]{:S(2)}) copy-start(f32[2,64,64]{2,1,0:T(8,128)} %impedance_ref.1) | copy-start | bytes 98308
  32.7 8.7 %all-to-all-start.2 = ((f32[16,2,128]{2,1,0:T(2,128)}), f32[16,2,128]{2,1,0:T(2,128)S(1)}, u32[]{:S(2)}, u32[]{:S(2)}) async-start(f32[16,2,128]{2,1,0:T(2,128)} %get-tuple-element.36), calls=%async_computation.2 | async-start | bytes 32768 | tf_op jit(solution)/shard_map/all_to_all | solution.py:727
where the time goes:
time: 42.7 us; the launch traced here: 42.3 us
  Pallas kernels  19.1 us (45%)
  starting transfers between devices  15.6 us (37%)
  waiting for transfers between devices  7.36 us (17%)
    all_to_all x1, starting transfers between devices, per_device(): lax.all_to_all(pack, 'chips', 0, 0, tiled=True, axis_index_groups=chip_me...  7.85 us
    pallas_call x1, Pallas kernels, per_device(): pl.pallas_call(near_kernel, out_shape=shape((2, tiles, width), F32), in_s...  4.88 us
    all_to_all x1, starting transfers between devices, per_device(): lax.all_to_all(coeff, ('chips', 'core'), 0, 0, tiled=True, axis_index_gro...  4.21 us
    pallas_call x1, Pallas kernels, per_device(): pl.pallas_call(own_lookup_kernel, out_shape=(shape((2, tiles, width), F32...  3.7 us
    all_to_all x1, starting transfers between devices, per_device(): lax.all_to_all(slots, ('chips', 'core'), 0, 0, tiled=True, axis_index_gro...  3.55 us
    pallas_call x1, Pallas kernels, per_device(): pl.pallas_call(functools.partial(voltage_kernel, first=own_rows), out_sha...  3.52 us
    all_to_all x1, waiting for transfers between devices, per_device(): lax.all_to_all(slots, ('chips', 'core'), 0, 0, tiled=True, axis_index_gro...  3.52 us
    pallas_call x1, Pallas kernels, per_device(): pl.pallas_call(functools.partial(current_kernel, first=own_rows), out_sha...  2.12 us
  transfers between devices with their start and end apart: 4, of which 4 were waited for; matrix products, arithmetic and copies ran while one was open for 0% of the time, Pallas kernels for 26%

commit v1 on v0

--- a/solution.py
+++ b/solution.py
@@ -36,7 +36,7 @@
 
 
 def turn(members):
-    return members // 4
+    return members // 2
 
 
 def chip_turn(chips):

time: 42.7 us -> 42.2 us (0.988)
  waiting for transfers between devices: 7.36 us -> 5.56 us
  starting transfers between devices: 15.6 us -> 16.9 us
    all_to_all x1, waiting for transfers between devices: 1.59 us -> 0.69 us  [per_device(): lax.all_to_all(coeff, ('chips', 'core'), 0, 0, tiled=True, axis_index_gro...]
    all_to_all x1, starting transfers between devices: 3.55 us -> 4.45 us  [per_device(): lax.all_to_all(slots, ('chips', 'core'), 0, 0, tiled=True, axis_index_gro...]
    all_to_all x1, waiting for transfers between devices: 3.52 us -> 2.62 us  [per_device(): lax.all_to_all(slots, ('chips', 'core'), 0, 0, tiled=True, axis_index_gro...]
where the time goes in v1:
time: 42.2 us; the launch traced here: 41.7 us
  Pallas kernels  19.1 us (45%)
  starting transfers between devices  16.9 us (40%)
  waiting for transfers between devices  5.56 us (13%)
    all_to_all x1, starting transfers between devices, per_device(): lax.all_to_all(pack, 'chips', 0, 0, tiled=True, axis_index_groups=chip_me...  7.85 us
    pallas_call x1, Pallas kernels, per_device(): pl.pallas_call(near_kernel, out_shape=shape((2, tiles, width), F32), in_s...  4.88 us
    all_to_all x1, starting transfers between devices, per_device(): lax.all_to_all(coeff, ('chips', 'core'), 0, 0, tiled=True, axis_index_gro...  4.57 us
    all_to_all x1, starting transfers between devices, per_device(): lax.all_to_all(slots, ('chips', 'core'), 0, 0, tiled=True, axis_index_gro...  4.45 us
    pallas_call x1, Pallas kernels, per_device(): pl.pallas_call(own_lookup_kernel, out_shape=(shape((2, tiles, width), F32...  3.7 us
    pallas_call x1, Pallas kernels, per_device(): pl.pallas_call(functools.partial(voltage_kernel, first=own_rows), out_sha...  3.52 us
    all_to_all x1, waiting for transfers between devices, per_device(): lax.all_to_all(slots, ('chips', 'core'), 0, 0, tiled=True, axis_index_gro...  2.62 us
    pallas_call x1, Pallas kernels, per_device(): pl.pallas_call(functools.partial(current_kernel, first=own_rows), out_sha...  2.12 us
  transfers between devices with their start and end apart: 4, of which 4 were waited for; matrix products, arithmetic and copies ran while one was open for 0% of the time, Pallas kernels for 26%

profile of v1, /device:TPU:0, one launch (start us, length us, event | category | flops | bytes accessed | tf_op | source)
XLA Modules:
  0.0 41.7 jit_solution(4102328349804270644)
XLA Ops:
  0.0 1.8 %pack.1 = (s16[8,80,128]{2,1,0:T(8,128)(2,1)}, f32[2,4096]{1,0:T(2,128)S(1)}, s32[16,128]{1,0:T(8,128)S(1)}, s32[1,64]{1,0:T(1,128)S(1)}, s32[2,64,128]{2,1,0:T(8,128)S(1)}) custom-call(f32[2,4096]{1,0:T(2,128)} %mesh_hbm.1, s32[16,128]{1,0:T(8,128)} %need_hbm.1, s32[1,64]{1,0:T(1,128)} %bitcast.15, s32[2,8192]{1,0:T(2,128)} %entry_hbm.1, s32[2,8192]{1,0:T(2,128)} %sign_hbm.1), custom_call_target="tpu_custom_call" | custom-call | tf_op jit(solution)/shard_map/pack/pallas_call | solution.py:603
  1.8 7.9 %all-to-all-start = ((s16[8,80,128]{2,1,0:T(8,128)(2,1)}), s16[8,80,128]{2,1,0:T(8,128)(2,1)S(1)}, u32[]{:S(2)}, u32[]{:S(2)}) async-start(s16[8,80,128]{2,1,0:T(8,128)(2,1)} %get-tuple-element.25), calls=%async_computation | async-start | bytes 327680 | tf_op jit(solution)/shard_map/all_to_all | solution.py:631
  9.6 0.0 copy-start.3
  9.6 3.7 %own_lookup.1 = (f32[2,64,128]{2,1,0:T(8,128)S(1)}, bf16[16,16,32,128]{3,2,1,0:T(8,128)(2,1)S(1)}) custom-call(f32[2,4096]{1,0:T(2,128)S(1)} %get-tuple-element.23.mesh_ref, s32[2,64,128]{2,1,0:T(8,128)S(1)} %get-tuple-element.22.code_ref, bf16[16,32,32,64]{3,2,1,0:T(8,128)(2,1)} %bitcast.11), custom_call_target="tpu_custom_call" | custom-call | flops 1000000000 | bytes 8000000 | tf_op jit(solution)/shard_map/own_lookup/pallas_call | solution.py:632
  13.3 1.5 %all-to-all-done.pack_hbm = s16[8,80,128]{2,1,0:T(8,128)(2,1)S(1)} async-done(((s16[8,80,128]{2,1,0:T(8,128)(2,1)}), s16[8,80,128]{2,1,0:T(8,128)(2,1)S(1)}, u32[]{:S(2)}, u32[]{:S(2)}) %all-to-all-start) | async-done | bytes 163872 | tf_op jit(solution)/shard_map/all_to_all | solution.py:631
  14.8 0.0 collective-permute-start
  14.8 0.6 %same_core.1 = (f32[2,64,128]{2,1,0:T(8,128)S(1)}, f32[2,8,128]{2,1,0:T(8,128)S(1)}) custom-call(f32[2,64,128]{2,1,0:T(8,128)S(1)} %get-tuple-element.24.part_hbm.part_ref, s16[8,80,128]{2,1,0:T(8,128)(2,1)S(1)} %hand_on.1.same_ref, s32[16,128]{1,0:T(8,128)S(1)} %get-tuple-element.26.need_ref, s32[2,64,128]{2,1,0:T(8,128)S(1)} %get-tuple-element.22.code_ref), custom_call_target="tpu_custom_call" | custom-call | flops 1000000000 | bytes 8000000 | tf_op jit(solution)/shard_map/same_core/pallas_call | solution.py:658
  15.5 0.8 %collective-permute-done.other_ref = s16[8,80,128]{2,1,0:T(8,128)(2,1)S(1)} collective-permute-done((s16[8,80,128]{2,1,0:T(8,128)(2,1)S(1)}, s16[8,80,128]{2,1,0:T(8,128)(2,1)S(1)}, u32[]{:S(2)}, u32[]{:S(2)}) %collective-permute-start) | collective-permute-done | bytes 163872 | tf_op jit(solution)/shard_map/ppermute | solution.py:657
  16.2 2.1 %currents.1 = (f32[2,64,128]{2,1,0:T(8,128)S(1)}, bf16[16,32,128]{2,1,0:T(8,128)(2,1)}, f32[2,8,128]{2,1,0:T(8,128)S(1)}) custom-call(f32[2,64,128]{2,1,0:T(8,128)S(1)} %get-tuple-element.27.part_ref, s16[8,80,128]{2,1,0:T(8,128)(2,1)S(1)} %collective-permute-done.other_ref, s32[16,128]{1,0:T(8,128)S(1)} %get-tuple-element.26.need_ref, ...), custom_call_target="tpu_custom_call" | custom-call | tf_op jit(solution)/shard_map/currents/pallas_call | solution.py:668
  18.4 4.6 %all-to-all-start.1 = ((bf16[16,32,128]{2,1,0:T(8,128)(2,1)}), bf16[16,32,128]{2,1,0:T(8,128)(2,1)S(1)}, u32[]{:S(2)}, u32[]{:S(2)}) async-start(bf16[16,32,128]{2,1,0:T(8,128)(2,1)} %get-tuple-element.28), calls=%async_computation.1 | async-start | bytes 262144 | tf_op jit(solution)/shard_map/all_to_all | solution.py:686
  22.9 0.0 copy-done.3
  22.9 0.1 add_add_fusion.source_ref
  23.0 0.0 copy-start
  23.0 0.0 copy-start.1
  23.0 0.0 copy-start.2
  23.0 4.9 %near_field.1.near_ref = f32[2,64,128]{2,1,0:T(8,128)S(1)} custom-call(s32[4,128]{1,0:T(4,128)S(1)} %add_add_fusion.source_ref, f32[2,64,128]{2,1,0:T(8,128)S(1)} %get-tuple-element.30.current_ref, f32[64,128]{1,0:T(8,128)} %bitcast.13, bf16[32768,128]{1,0:T(8,128)(2,1)} %bitcast.10), custom_call_target="tpu_custom_call" | custom-call | flops 1073741824 | bytes 8388608 | tf_op jit(solution)/shard_map/near_field/pallas_call | solution.py:690
  27.9 0.7 %all-to-all-done.1.coeff_ref = bf16[16,32,128]{2,1,0:T(8,128)(2,1)S(1)} async-done(((bf16[16,32,128]{2,1,0:T(8,128)(2,1)}), bf16[16,32,128]{2,1,0:T(8,128)(2,1)S(1)}, u32[]{:S(2)}, u32[]{:S(2)}) %all-to-all-start.1) | async-done | bytes 131104 | tf_op jit(solution)/shard_map/all_to_all | solution.py:686
  28.6 0.0 copy-done
  28.6 0.0 copy-done.1
  28.6 3.5 %voltages.1 = (f32[2,64,128]{2,1,0:T(8,128)S(1)}, f32[16,2,128]{2,1,0:T(2,128)}) custom-call(bf16[16,32,128]{2,1,0:T(8,128)(2,1)S(1)} %all-to-all-done.1.coeff_ref, s32[16,64]{1,0:T(8,128)S(1)} %bitcast.9, bf16[16,16,32,128]{3,2,1,0:T(8,128)(2,1)S(1)} %get-tuple-element.29.coupling_ref, bf16[2048,128]{1,0:T(8,128)(2,1)S(1)} %bitcast.8, ...), custom_call_target="tpu_custom_call" | custom-call | tf_op jit(solution)/shard_map/voltages/pallas_call | solution.py:707
  32.1 4.5 %all-to-all-start.2 = ((f32[16,2,128]{2,1,0:T(2,128)}), f32[16,2,128]{2,1,0:T(2,128)S(1)}, u32[]{:S(2)}, u32[]{:S(2)}) async-start(f32[16,2,128]{2,1,0:T(2,128)} %get-tuple-element.36), calls=%async_computation.2 | async-start | bytes 32768 | tf_op jit(solution)/shard_map/all_to_all | solution.py:727
  36.6 0.0 copy-done.2
  36.6 1.6 %own_sums.1 = (f32[2,32,128]{2,1,0:T(8,128)S(1)}, s32[2,8,128]{2,1,0:T(8,128)S(1)}, bf16[128,2048]{1,0:T(8,128)(2,1)S(1)}) custom-call(s32[2,64,128]{2,1,0:T(8,128)S(1)} %get-tuple-element.22.code_ref, f32[2,64,128]{2,1,0:T(8,128)S(1)} %get-tuple-element.31.voltage_ref, f32[2,8,128]{2,1,0:T(8,128)S(1)} %get-tuple-element.32.same_ref, ...), custom_call_target="tpu_custom_call" | custom-call | flops 1000000000 | bytes 8000000 | tf_op jit(solution)/shard_map/own_sums/pallas_call | solution.py:730
  38.2 2.6 %all-to-all-done.2.arrived_ref = f32[16,2,128]{2,1,0:T(2,128)S(1)} async-done(((f32[16,2,128]{2,1,0:T(2,128)}), f32[16,2,128]{2,1,0:T(2,128)S(1)}, u32[]{:S(2)}, u32[]{:S(2)}) %all-to-all-start.2) | async-done | bytes 16416 | tf_op jit(solution)/shard_map/all_to_all | solution.py:727
  40.8 0.9 %finish.1 = f32[2,4096]{1,0:T(2,128)} custom-call(f32[2,32,128]{2,1,0:T(8,128)S(1)} %get-tuple-element.35.own_ref, f32[16,2,128]{2,1,0:T(2,128)S(1)} %all-to-all-done.2.arrived_ref, s32[2,8,128]{2,1,0:T(8,128)S(1)} %get-tuple-element.37.asked_ref, bf16[128,2048]{1,0:T(8,128)(2,1)S(1)} %get-tuple-element.38.picks_ref), custom_call_target="tpu_custom_call" | custom-call | tf_op jit(solution)/shard_map/finish/pallas_call | solution.py:746
  (2 shorter events, 0.0 us)
Async XLA Ops:
  1.8 13.1 %all-to-all-start = ((s16[8,80,128]{2,1,0:T(8,128)(2,1)}), s16[8,80,128]{2,1,0:T(8,128)(2,1)S(1)}, u32[]{:S(2)}, u32[]{:S(2)}) async-start(s16[8,80,128]{2,1,0:T(8,128)(2,1)} %get-tuple-element.25), calls=%async_computation | async-start | bytes 327680 | tf_op jit(solution)/shard_map/all_to_all | solution.py:631
  9.6 13.3 %copy-start.3 = (s32[64,4]{0,1:T(4,128)S(1)}, s32[64,4]{0,1:T(4,128)}, u32[]{:S(2)}) copy-start(s32[64,4]{0,1:T(4,128)} %param.19) | copy-start | bytes 3076
  14.8 1.4 %collective-permute-start = (s16[8,80,128]{2,1,0:T(8,128)(2,1)S(1)}, s16[8,80,128]{2,1,0:T(8,128)(2,1)S(1)}, u32[]{:S(2)}, u32[]{:S(2)}) collective-permute-start(s16[8,80,128]{2,1,0:T(8,128)(2,1)S(1)} %hand_on.1.same_ref), channel_id=1, source_target_pairs={{0,1},{1,0},{2,3},{3,2},{4,5},{5,4},{6,7},{7,6},{8,9},{9,8},{10,11... | collective-permute-start | bytes 491528 | tf_op jit(solution)/shard_map/ppermute | solution.py:657
  18.4 10.2 %all-to-all-start.1 = ((bf16[16,32,128]{2,1,0:T(8,128)(2,1)}), bf16[16,32,128]{2,1,0:T(8,128)(2,1)S(1)}, u32[]{:S(2)}, u32[]{:S(2)}) async-start(bf16[16,32,128]{2,1,0:T(8,128)(2,1)} %get-tuple-element.28), calls=%async_computation.1 | async-start | bytes 262144 | tf_op jit(solution)/shard_map/all_to_all | solution.py:686
  23.0 5.6 %copy-start = (bf16[64,32,128]{2,1,0:T(8,128)(2,1)S(1)}, bf16[64,32,128]{2,1,0:T(8,128)(2,1)}, u32[]{:S(2)}) copy-start(bf16[64,32,128]{2,1,0:T(8,128)(2,1)} %param.22) | copy-start | bytes 1572868
  23.0 5.6 %copy-start.1 = (s32[64,16]{0,1:T(8,128)S(1)}, s32[64,16]{0,1:T(8,128)}, u32[]{:S(2)}) copy-start(s32[64,16]{0,1:T(8,128)} %param.23) | copy-start | bytes 12292
  23.0 13.6 %copy-start.2 = (f32[2,64,64]{2,1,0:T(8,128)S(1)}, f32[2,64,64]{2,1,0:T(8,128)}, u32[]{:S(2)}) copy-start(f32[2,64,64]{2,1,0:T(8,128)} %impedance_ref.1) | copy-start | bytes 98308
  32.1 8.7 %all-to-all-start.2 = ((f32[16,2,128]{2,1,0:T(2,128)}), f32[16,2,128]{2,1,0:T(2,128)S(1)}, u32[]{:S(2)}, u32[]{:S(2)}) async-start(f32[16,2,128]{2,1,0:T(2,128)} %get-tuple-element.36), calls=%async_computation.2 | async-start | bytes 32768 | tf_op jit(solution)/shard_map/all_to_all | solution.py:727

commit v2 on v1

--- a/solution.py
+++ b/solution.py
@@ -288,8 +288,8 @@
     tiles = current_ref.shape[1]
     width = blocks_ref.shape[1]
     count = blocks_ref.shape[0] // (tiles * width)
-    span = 8 * count * width
-    starts = [tiles * i // 64 for i in (0, 4, 8)]
+    span = 16 * count * width
+    starts = [0, tiles // 32, tiles // 16]
     copies = {}
     for i in range(2):
         rows = pl.ds(starts[i] * span, (starts[i + 1] - starts[i]) * span)
@@ -311,7 +311,7 @@
         ).astype(BF16)
     inputs = inputs_ref[...]
     total = jnp.zeros((width, 128), F32)
-    for g in range(tiles // 8):
+    for g in range(tiles // 16):
         if g in copies:
             copies[g].wait()
         block = jnp.concatenate(
@@ -319,7 +319,7 @@
                 jnp.concatenate(
                     [
                         blocks_ref[(t * count + k) * width : (t * count + k + 1) * width, :]
-                        for t in range(g * 8, g * 8 + 8)
+                        for t in range(g * 16, g * 16 + 16)
                     ],
                     axis=0,
                 )
@@ -328,9 +328,9 @@
             axis=1,
         )
         full = jnp.dot(block, inputs, preferred_element_type=F32)
-        for i in range(8):
+        for i in range(16):
             total = jnp.where(
-                lane_tile == g * 8 + i, full[i * width : (i + 1) * width], total
+                lane_tile == g * 16 + i, full[i * width : (i + 1) * width], total
             )
     rows = total.T
     late_copy.wait()
@@ -486,7 +486,7 @@
         voltage_ref[0, rows8, :] = near_ref[0, rows8, :] - far[8:16]
         voltage_ref[1, rows8, :] = near_ref[1, rows8, :] + far[0:8]
     sums = scatter(
-        code_ref, voltage_ref, spread_ref, first, slot_ref.shape[0], True
+        code_ref, voltage_ref, spread_ref, first, slot_ref.shape[0], False
     )
     shift = turn(peers)
     for c in range(2):

time: 42.2 us -> 42.2 us (level)
  no operation moved by 1% of the time
where the time goes in v2:
time: 42.2 us; the launch traced here: 41.8 us
  Pallas kernels  19.2 us (45%)
  starting transfers between devices  16.9 us (40%)
  waiting for transfers between devices  5.54 us (13%)
    all_to_all x1, starting transfers between devices, per_device(): lax.all_to_all(pack, 'chips', 0, 0, tiled=True, axis_index_groups=chip_me...  7.85 us
    pallas_call x1, Pallas kernels, per_device(): pl.pallas_call(near_kernel, out_shape=shape((2, tiles, width), F32), in_s...  4.9 us
    all_to_all x1, starting transfers between devices, per_device(): lax.all_to_all(coeff, ('chips', 'core'), 0, 0, tiled=True, axis_index_gro...  4.57 us
    all_to_all x1, starting transfers between devices, per_device(): lax.all_to_all(slots, ('chips', 'core'), 0, 0, tiled=True, axis_index_gro...  4.47 us
    pallas_call x1, Pallas kernels, per_device(): pl.pallas_call(own_lookup_kernel, out_shape=(shape((2, tiles, width), F32...  3.7 us
    pallas_call x1, Pallas kernels, per_device(): pl.pallas_call(functools.partial(voltage_kernel, first=own_rows), out_sha...  3.56 us
    all_to_all x1, waiting for transfers between devices, per_device(): lax.all_to_all(slots, ('chips', 'core'), 0, 0, tiled=True, axis_index_gro...  2.62 us
    pallas_call x1, Pallas kernels, per_device(): pl.pallas_call(functools.partial(current_kernel, first=own_rows), out_sha...  2.12 us
  transfers between devices with their start and end apart: 4, of which 4 were waited for; matrix products, arithmetic and copies ran while one was open for 0% of the time, Pallas kernels for 26%

profile of v2, /device:TPU:0, one launch (start us, length us, event | category | flops | bytes accessed | tf_op | source)
XLA Modules:
  0.0 41.8 jit_solution(12411843298349059057)
XLA Ops:
  0.0 1.8 %pack.1 = (s16[8,80,128]{2,1,0:T(8,128)(2,1)}, f32[2,4096]{1,0:T(2,128)S(1)}, s32[16,128]{1,0:T(8,128)S(1)}, s32[1,64]{1,0:T(1,128)S(1)}, s32[2,64,128]{2,1,0:T(8,128)S(1)}) custom-call(f32[2,4096]{1,0:T(2,128)} %mesh_hbm.1, s32[16,128]{1,0:T(8,128)} %need_hbm.1, s32[1,64]{1,0:T(1,128)} %bitcast.15, s32[2,8192]{1,0:T(2,128)} %entry_hbm.1, s32[2,8192]{1,0:T(2,128)} %sign_hbm.1), custom_call_target="tpu_custom_call" | custom-call | tf_op jit(solution)/shard_map/pack/pallas_call | solution.py:603
  1.8 7.9 %all-to-all-start = ((s16[8,80,128]{2,1,0:T(8,128)(2,1)}), s16[8,80,128]{2,1,0:T(8,128)(2,1)S(1)}, u32[]{:S(2)}, u32[]{:S(2)}) async-start(s16[8,80,128]{2,1,0:T(8,128)(2,1)} %get-tuple-element.25), calls=%async_computation | async-start | bytes 327680 | tf_op jit(solution)/shard_map/all_to_all | solution.py:631
  9.6 0.0 copy-start.3
  9.6 3.7 %own_lookup.1 = (f32[2,64,128]{2,1,0:T(8,128)S(1)}, bf16[16,16,32,128]{3,2,1,0:T(8,128)(2,1)S(1)}) custom-call(f32[2,4096]{1,0:T(2,128)S(1)} %get-tuple-element.23.mesh_ref, s32[2,64,128]{2,1,0:T(8,128)S(1)} %get-tuple-element.22.code_ref, bf16[16,32,32,64]{3,2,1,0:T(8,128)(2,1)} %bitcast.11), custom_call_target="tpu_custom_call" | custom-call | flops 1000000000 | bytes 8000000 | tf_op jit(solution)/shard_map/own_lookup/pallas_call | solution.py:632
  13.3 1.5 %all-to-all-done.pack_hbm = s16[8,80,128]{2,1,0:T(8,128)(2,1)S(1)} async-done(((s16[8,80,128]{2,1,0:T(8,128)(2,1)}), s16[8,80,128]{2,1,0:T(8,128)(2,1)S(1)}, u32[]{:S(2)}, u32[]{:S(2)}) %all-to-all-start) | async-done | bytes 163872 | tf_op jit(solution)/shard_map/all_to_all | solution.py:631
  14.8 0.0 collective-permute-start
  14.8 0.6 %same_core.1 = (f32[2,64,128]{2,1,0:T(8,128)S(1)}, f32[2,8,128]{2,1,0:T(8,128)S(1)}) custom-call(f32[2,64,128]{2,1,0:T(8,128)S(1)} %get-tuple-element.24.part_hbm.part_ref, s16[8,80,128]{2,1,0:T(8,128)(2,1)S(1)} %hand_on.1.same_ref, s32[16,128]{1,0:T(8,128)S(1)} %get-tuple-element.26.need_ref, s32[2,64,128]{2,1,0:T(8,128)S(1)} %get-tuple-element.22.code_ref), custom_call_target="tpu_custom_call" | custom-call | flops 1000000000 | bytes 8000000 | tf_op jit(solution)/shard_map/same_core/pallas_call | solution.py:658
  15.5 0.8 %collective-permute-done.other_ref = s16[8,80,128]{2,1,0:T(8,128)(2,1)S(1)} collective-permute-done((s16[8,80,128]{2,1,0:T(8,128)(2,1)S(1)}, s16[8,80,128]{2,1,0:T(8,128)(2,1)S(1)}, u32[]{:S(2)}, u32[]{:S(2)}) %collective-permute-start) | collective-permute-done | bytes 163872 | tf_op jit(solution)/shard_map/ppermute | solution.py:657
  16.2 2.1 %currents.1 = (f32[2,64,128]{2,1,0:T(8,128)S(1)}, bf16[16,32,128]{2,1,0:T(8,128)(2,1)}, f32[2,8,128]{2,1,0:T(8,128)S(1)}) custom-call(f32[2,64,128]{2,1,0:T(8,128)S(1)} %get-tuple-element.27.part_ref, s16[8,80,128]{2,1,0:T(8,128)(2,1)S(1)} %collective-permute-done.other_ref, s32[16,128]{1,0:T(8,128)S(1)} %get-tuple-element.26.need_ref, ...), custom_call_target="tpu_custom_call" | custom-call | tf_op jit(solution)/shard_map/currents/pallas_call | solution.py:668
  18.4 4.6 %all-to-all-start.1 = ((bf16[16,32,128]{2,1,0:T(8,128)(2,1)}), bf16[16,32,128]{2,1,0:T(8,128)(2,1)S(1)}, u32[]{:S(2)}, u32[]{:S(2)}) async-start(bf16[16,32,128]{2,1,0:T(8,128)(2,1)} %get-tuple-element.28), calls=%async_computation.1 | async-start | bytes 262144 | tf_op jit(solution)/shard_map/all_to_all | solution.py:686
  22.9 0.0 copy-done.3
  22.9 0.1 add_add_fusion.source_ref
  23.0 0.0 copy-start
  23.0 0.0 copy-start.1
  23.0 0.0 copy-start.2
  23.0 4.9 %near_field.1.near_ref = f32[2,64,128]{2,1,0:T(8,128)S(1)} custom-call(s32[4,128]{1,0:T(4,128)S(1)} %add_add_fusion.source_ref, f32[2,64,128]{2,1,0:T(8,128)S(1)} %get-tuple-element.30.current_ref, f32[64,128]{1,0:T(8,128)} %bitcast.13, bf16[32768,128]{1,0:T(8,128)(2,1)} %bitcast.10), custom_call_target="tpu_custom_call" | custom-call | flops 1073741824 | bytes 8388608 | tf_op jit(solution)/shard_map/near_field/pallas_call | solution.py:690
  27.9 0.7 %all-to-all-done.1.coeff_ref = bf16[16,32,128]{2,1,0:T(8,128)(2,1)S(1)} async-done(((bf16[16,32,128]{2,1,0:T(8,128)(2,1)}), bf16[16,32,128]{2,1,0:T(8,128)(2,1)S(1)}, u32[]{:S(2)}, u32[]{:S(2)}) %all-to-all-start.1) | async-done | bytes 131104 | tf_op jit(solution)/shard_map/all_to_all | solution.py:686
  28.6 0.0 copy-done
  28.6 0.0 copy-done.1
  28.6 3.6 %voltages.1 = (f32[2,64,128]{2,1,0:T(8,128)S(1)}, f32[16,2,128]{2,1,0:T(2,128)}) custom-call(bf16[16,32,128]{2,1,0:T(8,128)(2,1)S(1)} %all-to-all-done.1.coeff_ref, s32[16,64]{1,0:T(8,128)S(1)} %bitcast.9, bf16[16,16,32,128]{3,2,1,0:T(8,128)(2,1)S(1)} %get-tuple-element.29.coupling_ref, bf16[2048,128]{1,0:T(8,128)(2,1)S(1)} %bitcast.8, ...), custom_call_target="tpu_custom_call" | custom-call | tf_op jit(solution)/shard_map/voltages/pallas_call | solution.py:707
  32.2 4.5 %all-to-all-start.2 = ((f32[16,2,128]{2,1,0:T(2,128)}), f32[16,2,128]{2,1,0:T(2,128)S(1)}, u32[]{:S(2)}, u32[]{:S(2)}) async-start(f32[16,2,128]{2,1,0:T(2,128)} %get-tuple-element.36), calls=%async_computation.2 | async-start | bytes 32768 | tf_op jit(solution)/shard_map/all_to_all | solution.py:727
  36.6 0.0 copy-done.2
  36.6 1.6 %own_sums.1 = (f32[2,32,128]{2,1,0:T(8,128)S(1)}, s32[2,8,128]{2,1,0:T(8,128)S(1)}, bf16[128,2048]{1,0:T(8,128)(2,1)S(1)}) custom-call(s32[2,64,128]{2,1,0:T(8,128)S(1)} %get-tuple-element.22.code_ref, f32[2,64,128]{2,1,0:T(8,128)S(1)} %get-tuple-element.31.voltage_ref, f32[2,8,128]{2,1,0:T(8,128)S(1)} %get-tuple-element.32.same_ref, ...), custom_call_target="tpu_custom_call" | custom-call | flops 1000000000 | bytes 8000000 | tf_op jit(solution)/shard_map/own_sums/pallas_call | solution.py:730
  38.2 2.6 %all-to-all-done.2.arrived_ref = f32[16,2,128]{2,1,0:T(2,128)S(1)} async-done(((f32[16,2,128]{2,1,0:T(2,128)}), f32[16,2,128]{2,1,0:T(2,128)S(1)}, u32[]{:S(2)}, u32[]{:S(2)}) %all-to-all-start.2) | async-done | bytes 16416 | tf_op jit(solution)/shard_map/all_to_all | solution.py:727
  40.9 0.9 %finish.1 = f32[2,4096]{1,0:T(2,128)} custom-call(f32[2,32,128]{2,1,0:T(8,128)S(1)} %get-tuple-element.35.own_ref, f32[16,2,128]{2,1,0:T(2,128)S(1)} %all-to-all-done.2.arrived_ref, s32[2,8,128]{2,1,0:T(8,128)S(1)} %get-tuple-element.37.asked_ref, bf16[128,2048]{1,0:T(8,128)(2,1)S(1)} %get-tuple-element.38.picks_ref), custom_call_target="tpu_custom_call" | custom-call | tf_op jit(solution)/shard_map/finish/pallas_call | solution.py:746
  (2 shorter events, 0.0 us)
Async XLA Ops:
  1.8 13.1 %all-to-all-start = ((s16[8,80,128]{2,1,0:T(8,128)(2,1)}), s16[8,80,128]{2,1,0:T(8,128)(2,1)S(1)}, u32[]{:S(2)}, u32[]{:S(2)}) async-start(s16[8,80,128]{2,1,0:T(8,128)(2,1)} %get-tuple-element.25), calls=%async_computation | async-start | bytes 327680 | tf_op jit(solution)/shard_map/all_to_all | solution.py:631
  9.6 13.3 %copy-start.3 = (s32[64,4]{0,1:T(4,128)S(1)}, s32[64,4]{0,1:T(4,128)}, u32[]{:S(2)}) copy-start(s32[64,4]{0,1:T(4,128)} %param.19) | copy-start | bytes 3076
  14.8 1.4 %collective-permute-start = (s16[8,80,128]{2,1,0:T(8,128)(2,1)S(1)}, s16[8,80,128]{2,1,0:T(8,128)(2,1)S(1)}, u32[]{:S(2)}, u32[]{:S(2)}) collective-permute-start(s16[8,80,128]{2,1,0:T(8,128)(2,1)S(1)} %hand_on.1.same_ref), channel_id=1, source_target_pairs={{0,1},{1,0},{2,3},{3,2},{4,5},{5,4},{6,7},{7,6},{8,9},{9,8},{10,11... | collective-permute-start | bytes 491528 | tf_op jit(solution)/shard_map/ppermute | solution.py:657
  18.4 10.2 %all-to-all-start.1 = ((bf16[16,32,128]{2,1,0:T(8,128)(2,1)}), bf16[16,32,128]{2,1,0:T(8,128)(2,1)S(1)}, u32[]{:S(2)}, u32[]{:S(2)}) async-start(bf16[16,32,128]{2,1,0:T(8,128)(2,1)} %get-tuple-element.28), calls=%async_computation.1 | async-start | bytes 262144 | tf_op jit(solution)/shard_map/all_to_all | solution.py:686
  23.0 5.6 %copy-start = (bf16[64,32,128]{2,1,0:T(8,128)(2,1)S(1)}, bf16[64,32,128]{2,1,0:T(8,128)(2,1)}, u32[]{:S(2)}) copy-start(bf16[64,32,128]{2,1,0:T(8,128)(2,1)} %param.22) | copy-start | bytes 1572868
  23.0 5.6 %copy-start.1 = (s32[64,16]{0,1:T(8,128)S(1)}, s32[64,16]{0,1:T(8,128)}, u32[]{:S(2)}) copy-start(s32[64,16]{0,1:T(8,128)} %param.23) | copy-start | bytes 12292
  23.0 13.6 %copy-start.2 = (f32[2,64,64]{2,1,0:T(8,128)S(1)}, f32[2,64,64]{2,1,0:T(8,128)}, u32[]{:S(2)}) copy-start(f32[2,64,64]{2,1,0:T(8,128)} %impedance_ref.1) | copy-start | bytes 98308
  32.2 8.7 %all-to-all-start.2 = ((f32[16,2,128]{2,1,0:T(2,128)}), f32[16,2,128]{2,1,0:T(2,128)S(1)}, u32[]{:S(2)}, u32[]{:S(2)}) async-start(f32[16,2,128]{2,1,0:T(2,128)} %get-tuple-element.36), calls=%async_computation.2 | async-start | bytes 32768 | tf_op jit(solution)/shard_map/all_to_all | solution.py:727

commit v3 on v1

--- a/solution.py
+++ b/solution.py
@@ -297,9 +297,10 @@
             blocks_hbm.at[rows], blocks_ref.at[rows], sems.at[i]
         )
     late_copy = pltpu.make_async_copy(resistance_hbm, resistance_ref, sems.at[2])
-    for copy in copies.values():
-        copy.start()
+    copies[starts[0]].start()
     late_copy.start()
+    late_copy.wait()
+    copies[starts[1]].start()
     lane_tile = lax.broadcasted_iota(jnp.int32, (width, 128), 1) % tiles
     rows = jnp.concatenate([current_ref[0], current_ref[1]], axis=0)
     columns = rows.T.astype(BF16)
@@ -333,7 +334,6 @@
                 lane_tile == g * 8 + i, full[i * width : (i + 1) * width], total
             )
     rows = total.T
-    late_copy.wait()
     resistance = resistance_ref[...]
     out_ref[0] = resistance * current_ref[0] - rows[tiles:]
     out_ref[1] = resistance * current_ref[1] + rows[:tiles]

time: 42.2 us -> 43 us (1.019)
  Pallas kernels: 19.1 us -> 19.9 us
  waiting for transfers between devices: 5.56 us -> 4.87 us
  starting transfers between devices: 16.9 us -> 17.5 us
    pallas_call x1, Pallas kernels: 4.88 us -> 5.67 us  [per_device(): pl.pallas_call(near_kernel, out_shape=shape((2, tiles, width), F32), in_s...]
    all_to_all x1, waiting for transfers between devices: 0.69 us -> 0.01 us  [per_device(): lax.all_to_all(coeff, ('chips', 'core'), 0, 0, tiled=True, axis_index_gro...]
    all_to_all x1, starting transfers between devices: 4.45 us -> 5.12 us  [per_device(): lax.all_to_all(slots, ('chips', 'core'), 0, 0, tiled=True, axis_index_gro...]
  transfers between devices with their start and end apart: 4 -> 4, of which waited for: 4 -> 3; matrix products, arithmetic and copies ran while one was open for 0% -> 0% of each run, Pallas kernels for 26% -> 27%
where the time goes in v3:
time: 43 us; the launch traced here: 42.5 us
  Pallas kernels  19.9 us (46%)
  starting transfers between devices  17.5 us (41%)
  waiting for transfers between devices  4.87 us (11%)
    all_to_all x1, starting transfers between devices, per_device(): lax.all_to_all(pack, 'chips', 0, 0, tiled=True, axis_index_groups=chip_me...  7.85 us
    pallas_call x1, Pallas kernels, per_device(): pl.pallas_call(near_kernel, out_shape=shape((2, tiles, width), F32), in_s...  5.67 us
    all_to_all x1, starting transfers between devices, per_device(): lax.all_to_all(slots, ('chips', 'core'), 0, 0, tiled=True, axis_index_gro...  5.12 us
    all_to_all x1, starting transfers between devices, per_device(): lax.all_to_all(coeff, ('chips', 'core'), 0, 0, tiled=True, axis_index_gro...  4.57 us
    pallas_call x1, Pallas kernels, per_device(): pl.pallas_call(own_lookup_kernel, out_shape=(shape((2, tiles, width), F32...  3.7 us
    pallas_call x1, Pallas kernels, per_device(): pl.pallas_call(functools.partial(voltage_kernel, first=own_rows), out_sha...  3.53 us
    all_to_all x1, waiting for transfers between devices, per_device(): lax.all_to_all(slots, ('chips', 'core'), 0, 0, tiled=True, axis_index_gro...  2.62 us
    pallas_call x1, Pallas kernels, per_device(): pl.pallas_call(functools.partial(current_kernel, first=own_rows), out_sha...  2.12 us
  transfers between devices with their start and end apart: 4, of which 3 were waited for; matrix products, arithmetic and copies ran while one was open for 0% of the time, Pallas kernels for 27%

profile of v3, /device:TPU:0, one launch (start us, length us, event | category | flops | bytes accessed | tf_op | source)
XLA Modules:
  0.0 42.5 jit_solution(5854733509187032093)
XLA Ops:
  0.0 1.8 %pack.1 = (s16[8,80,128]{2,1,0:T(8,128)(2,1)}, f32[2,4096]{1,0:T(2,128)S(1)}, s32[16,128]{1,0:T(8,128)S(1)}, s32[1,64]{1,0:T(1,128)S(1)}, s32[2,64,128]{2,1,0:T(8,128)S(1)}) custom-call(f32[2,4096]{1,0:T(2,128)} %mesh_hbm.1, s32[16,128]{1,0:T(8,128)} %need_hbm.1, s32[1,64]{1,0:T(1,128)} %bitcast.15, s32[2,8192]{1,0:T(2,128)} %entry_hbm.1, s32[2,8192]{1,0:T(2,128)} %sign_hbm.1), custom_call_target="tpu_custom_call" | custom-call | tf_op jit(solution)/shard_map/pack/pallas_call | solution.py:603
  1.8 7.9 %all-to-all-start = ((s16[8,80,128]{2,1,0:T(8,128)(2,1)}), s16[8,80,128]{2,1,0:T(8,128)(2,1)S(1)}, u32[]{:S(2)}, u32[]{:S(2)}) async-start(s16[8,80,128]{2,1,0:T(8,128)(2,1)} %get-tuple-element.25), calls=%async_computation | async-start | bytes 327680 | tf_op jit(solution)/shard_map/all_to_all | solution.py:631
  9.6 0.0 copy-start.3
  9.6 3.7 %own_lookup.1 = (f32[2,64,128]{2,1,0:T(8,128)S(1)}, bf16[16,16,32,128]{3,2,1,0:T(8,128)(2,1)S(1)}) custom-call(f32[2,4096]{1,0:T(2,128)S(1)} %get-tuple-element.23.mesh_ref, s32[2,64,128]{2,1,0:T(8,128)S(1)} %get-tuple-element.22.code_ref, bf16[16,32,32,64]{3,2,1,0:T(8,128)(2,1)} %bitcast.11), custom_call_target="tpu_custom_call" | custom-call | flops 1000000000 | bytes 8000000 | tf_op jit(solution)/shard_map/own_lookup/pallas_call | solution.py:632
  13.3 1.5 %all-to-all-done.pack_hbm = s16[8,80,128]{2,1,0:T(8,128)(2,1)S(1)} async-done(((s16[8,80,128]{2,1,0:T(8,128)(2,1)}), s16[8,80,128]{2,1,0:T(8,128)(2,1)S(1)}, u32[]{:S(2)}, u32[]{:S(2)}) %all-to-all-start) | async-done | bytes 163872 | tf_op jit(solution)/shard_map/all_to_all | solution.py:631
  14.8 0.0 collective-permute-start
  14.8 0.6 %same_core.1 = (f32[2,64,128]{2,1,0:T(8,128)S(1)}, f32[2,8,128]{2,1,0:T(8,128)S(1)}) custom-call(f32[2,64,128]{2,1,0:T(8,128)S(1)} %get-tuple-element.24.part_hbm.part_ref, s16[8,80,128]{2,1,0:T(8,128)(2,1)S(1)} %hand_on.1.same_ref, s32[16,128]{1,0:T(8,128)S(1)} %get-tuple-element.26.need_ref, s32[2,64,128]{2,1,0:T(8,128)S(1)} %get-tuple-element.22.code_ref), custom_call_target="tpu_custom_call" | custom-call | flops 1000000000 | bytes 8000000 | tf_op jit(solution)/shard_map/same_core/pallas_call | solution.py:658
  15.5 0.8 %collective-permute-done.other_ref = s16[8,80,128]{2,1,0:T(8,128)(2,1)S(1)} collective-permute-done((s16[8,80,128]{2,1,0:T(8,128)(2,1)S(1)}, s16[8,80,128]{2,1,0:T(8,128)(2,1)S(1)}, u32[]{:S(2)}, u32[]{:S(2)}) %collective-permute-start) | collective-permute-done | bytes 163872 | tf_op jit(solution)/shard_map/ppermute | solution.py:657
  16.2 2.1 %currents.1 = (f32[2,64,128]{2,1,0:T(8,128)S(1)}, bf16[16,32,128]{2,1,0:T(8,128)(2,1)}, f32[2,8,128]{2,1,0:T(8,128)S(1)}) custom-call(f32[2,64,128]{2,1,0:T(8,128)S(1)} %get-tuple-element.27.part_ref, s16[8,80,128]{2,1,0:T(8,128)(2,1)S(1)} %collective-permute-done.other_ref, s32[16,128]{1,0:T(8,128)S(1)} %get-tuple-element.26.need_ref, ...), custom_call_target="tpu_custom_call" | custom-call | tf_op jit(solution)/shard_map/currents/pallas_call | solution.py:668
  18.4 4.6 %all-to-all-start.1 = ((bf16[16,32,128]{2,1,0:T(8,128)(2,1)}), bf16[16,32,128]{2,1,0:T(8,128)(2,1)S(1)}, u32[]{:S(2)}, u32[]{:S(2)}) async-start(bf16[16,32,128]{2,1,0:T(8,128)(2,1)} %get-tuple-element.28), calls=%async_computation.1 | async-start | bytes 262144 | tf_op jit(solution)/shard_map/all_to_all | solution.py:686
  22.9 0.0 copy-done.3
  22.9 0.1 add_add_fusion.source_ref
  23.0 0.0 copy-start
  23.0 0.0 copy-start.1
  23.0 0.0 copy-start.2
  23.0 5.7 %near_field.1.near_ref = f32[2,64,128]{2,1,0:T(8,128)S(1)} custom-call(s32[4,128]{1,0:T(4,128)S(1)} %add_add_fusion.source_ref, f32[2,64,128]{2,1,0:T(8,128)S(1)} %get-tuple-element.30.current_ref, f32[64,128]{1,0:T(8,128)} %bitcast.13, bf16[32768,128]{1,0:T(8,128)(2,1)} %bitcast.10), custom_call_target="tpu_custom_call" | custom-call | flops 1073741824 | bytes 8388608 | tf_op jit(solution)/shard_map/near_field/pallas_call | solution.py:690
  28.7 0.0 all-to-all-done.1.coeff_ref
  28.7 0.0 copy-done
  28.7 0.0 copy-done.1
  28.7 3.5 %voltages.1 = (f32[2,64,128]{2,1,0:T(8,128)S(1)}, f32[16,2,128]{2,1,0:T(2,128)}) custom-call(bf16[16,32,128]{2,1,0:T(8,128)(2,1)S(1)} %all-to-all-done.1.coeff_ref, s32[16,64]{1,0:T(8,128)S(1)} %bitcast.9, bf16[16,16,32,128]{3,2,1,0:T(8,128)(2,1)S(1)} %get-tuple-element.29.coupling_ref, bf16[2048,128]{1,0:T(8,128)(2,1)S(1)} %bitcast.8, ...), custom_call_target="tpu_custom_call" | custom-call | tf_op jit(solution)/shard_map/voltages/pallas_call | solution.py:707
  32.2 5.1 %all-to-all-start.2 = ((f32[16,2,128]{2,1,0:T(2,128)}), f32[16,2,128]{2,1,0:T(2,128)S(1)}, u32[]{:S(2)}, u32[]{:S(2)}) async-start(f32[16,2,128]{2,1,0:T(2,128)} %get-tuple-element.36), calls=%async_computation.2 | async-start | bytes 32768 | tf_op jit(solution)/shard_map/all_to_all | solution.py:727
  37.4 0.0 copy-done.2
  37.4 1.6 %own_sums.1 = (f32[2,32,128]{2,1,0:T(8,128)S(1)}, s32[2,8,128]{2,1,0:T(8,128)S(1)}, bf16[128,2048]{1,0:T(8,128)(2,1)S(1)}) custom-call(s32[2,64,128]{2,1,0:T(8,128)S(1)} %get-tuple-element.22.code_ref, f32[2,64,128]{2,1,0:T(8,128)S(1)} %get-tuple-element.31.voltage_ref, f32[2,8,128]{2,1,0:T(8,128)S(1)} %get-tuple-element.32.same_ref, ...), custom_call_target="tpu_custom_call" | custom-call | flops 1000000000 | bytes 8000000 | tf_op jit(solution)/shard_map/own_sums/pallas_call | solution.py:730
  39.0 2.6 %all-to-all-done.2.arrived_ref = f32[16,2,128]{2,1,0:T(2,128)S(1)} async-done(((f32[16,2,128]{2,1,0:T(2,128)}), f32[16,2,128]{2,1,0:T(2,128)S(1)}, u32[]{:S(2)}, u32[]{:S(2)}) %all-to-all-start.2) | async-done | bytes 16416 | tf_op jit(solution)/shard_map/all_to_all | solution.py:727
  41.6 0.9 %finish.1 = f32[2,4096]{1,0:T(2,128)} custom-call(f32[2,32,128]{2,1,0:T(8,128)S(1)} %get-tuple-element.35.own_ref, f32[16,2,128]{2,1,0:T(2,128)S(1)} %all-to-all-done.2.arrived_ref, s32[2,8,128]{2,1,0:T(8,128)S(1)} %get-tuple-element.37.asked_ref, bf16[128,2048]{1,0:T(8,128)(2,1)S(1)} %get-tuple-element.38.picks_ref), custom_call_target="tpu_custom_call" | custom-call | tf_op jit(solution)/shard_map/finish/pallas_call | solution.py:746
  (2 shorter events, 0.0 us)
Async XLA Ops:
  1.8 13.1 %all-to-all-start = ((s16[8,80,128]{2,1,0:T(8,128)(2,1)}), s16[8,80,128]{2,1,0:T(8,128)(2,1)S(1)}, u32[]{:S(2)}, u32[]{:S(2)}) async-start(s16[8,80,128]{2,1,0:T(8,128)(2,1)} %get-tuple-element.25), calls=%async_computation | async-start | bytes 327680 | tf_op jit(solution)/shard_map/all_to_all | solution.py:631
  9.6 13.3 %copy-start.3 = (s32[64,4]{0,1:T(4,128)S(1)}, s32[64,4]{0,1:T(4,128)}, u32[]{:S(2)}) copy-start(s32[64,4]{0,1:T(4,128)} %param.19) | copy-start | bytes 3076
  14.8 1.4 %collective-permute-start = (s16[8,80,128]{2,1,0:T(8,128)(2,1)S(1)}, s16[8,80,128]{2,1,0:T(8,128)(2,1)S(1)}, u32[]{:S(2)}, u32[]{:S(2)}) collective-permute-start(s16[8,80,128]{2,1,0:T(8,128)(2,1)S(1)} %hand_on.1.same_ref), channel_id=1, source_target_pairs={{0,1},{1,0},{2,3},{3,2},{4,5},{5,4},{6,7},{7,6},{8,9},{9,8},{10,11... | collective-permute-start | bytes 491528 | tf_op jit(solution)/shard_map/ppermute | solution.py:657
  18.4 10.3 %all-to-all-start.1 = ((bf16[16,32,128]{2,1,0:T(8,128)(2,1)}), bf16[16,32,128]{2,1,0:T(8,128)(2,1)S(1)}, u32[]{:S(2)}, u32[]{:S(2)}) async-start(bf16[16,32,128]{2,1,0:T(8,128)(2,1)} %get-tuple-element.28), calls=%async_computation.1 | async-start | bytes 262144 | tf_op jit(solution)/shard_map/all_to_all | solution.py:686
  23.0 5.7 %copy-start = (bf16[64,32,128]{2,1,0:T(8,128)(2,1)S(1)}, bf16[64,32,128]{2,1,0:T(8,128)(2,1)}, u32[]{:S(2)}) copy-start(bf16[64,32,128]{2,1,0:T(8,128)(2,1)} %param.22) | copy-start | bytes 1572868
  23.0 5.7 %copy-start.1 = (s32[64,16]{0,1:T(8,128)S(1)}, s32[64,16]{0,1:T(8,128)}, u32[]{:S(2)}) copy-start(s32[64,16]{0,1:T(8,128)} %param.23) | copy-start | bytes 12292
  23.0 14.4 %copy-start.2 = (f32[2,64,64]{2,1,0:T(8,128)S(1)}, f32[2,64,64]{2,1,0:T(8,128)}, u32[]{:S(2)}) copy-start(f32[2,64,64]{2,1,0:T(8,128)} %impedance_ref.1) | copy-start | bytes 98308
  32.2 9.3 %all-to-all-start.2 = ((f32[16,2,128]{2,1,0:T(2,128)}), f32[16,2,128]{2,1,0:T(2,128)S(1)}, u32[]{:S(2)}, u32[]{:S(2)}) async-start(f32[16,2,128]{2,1,0:T(2,128)} %get-tuple-element.36), calls=%async_computation.2 | async-start | bytes 32768 | tf_op jit(solution)/shard_map/all_to_all | solution.py:727
